TPU v7x, 32 devices: a whole 2x2x4 slice. The times are simulated.
32 devices in a mesh: rep: 16 (over z, y, core), voc: 2 (over x).
Axes of the slice: x: 2, y: 2, z: 4, core: 2. Of those that a mesh axis runs over, the one named last changes fastest.
Arguments:
- states: bfloat16 [2, 256, 6144], P(None, None, 'rep'), may hold values from -6 to 6
- head_weight: bfloat16 [6144, 4096], P('rep', 'voc'), may hold values from -0.21875 to 0.21875
- pair_order: int32 [2, 8], replicated, may hold values from 0 to 7, each once within a row
- row_example: int32 [2, 8, 256], replicated, may hold values from 0 to 255, each once within a row
Outputs:
- state_grad: bfloat16 [2, 256, 6144], P(None, None, 'rep')
- head_grad: bfloat16 [6144, 4096], P('rep', 'voc')
Inputs may be any that keep to these rules, and one draw needn't show every extreme that they name: Each row pair_order[m] holds every replica once. Each row row_example[m, r] holds every number of 0 to 255 once.
All inputs are finite; a program needn't handle non-finite values.
Results may differ from a plain program's by a relative error of at most 0.0055.
Values may be sent and summed in bfloat16 or wider, within the bound.
No kernel may reach another device: no remote copies, remote signals or barrier semaphores. Data moves between devices by JAX's collectives and lax.ppermute only.
A program may use at most 64 MiB of HBM per device.

v0:
```python
import functools
import itertools
import math

import jax
import jax.numpy as jnp
from jax import lax
from jax.experimental import pallas as pl
from jax.experimental.pallas import tpu as pltpu
from jax.sharding import PartitionSpec as P

distill_weight = 0.0625
max_permutations = 24
head_parts = 4


def partner_table(pair_order):
    slot_count = pair_order.shape[1]
    slot_ids = jnp.arange(slot_count, dtype=jnp.int32)
    matches = pair_order[:, None, :] == slot_ids[None, :, None]
    following = jnp.roll(pair_order, -1, axis=1)
    return jnp.sum(jnp.where(matches, following[:, None, :], 0), axis=2)


def route_kernel(order_ref, *refs):
    *branch_refs, flags_ref, dest, src, color = refs
    micro_count, replicas = order_ref.shape
    pairs = replicas // 2
    replica = lax.axis_index("rep") // 2
    for m in range(micro_count):
        for k in range(replicas):
            to, frm = order_ref[m, k], order_ref[m, (k + 1) % replicas]
            dest[frm] = to
            src[to] = frm
            color[k] = -1
        for start in range(0, replicas, 2):
            at = jnp.where(color[start] == 1, start + 1, start)
            for _ in range(pairs):
                color[at] = 0
                color[at ^ 1] = 1
                at = src[dest[at ^ 1] ^ 1]
        for c in range(2):
            sigma = []
            place = jnp.int32(0)
            for z in range(pairs):
                leaves = jnp.where(color[2 * z] == c, 2 * z, 2 * z + 1)
                to = dest[leaves] // 2
                smaller = to
                for earlier in sigma:
                    smaller = smaller - jnp.where(earlier < to, 1, 0)
                place = place * (pairs - z) + smaller
                sigma.append(to)
            branch_refs[2 * m + c][0] = place
        for row, moved in enumerate((replica, src[replica])):
            at = 2 * m + row
            flags_ref[at : at + 1, :] = jnp.full((1, flags_ref.shape[1]), color[moved], jnp.int32)


def routes(pair_order, width):
    micro_count, replicas = pair_order.shape
    smem = pl.BlockSpec(memory_space=pltpu.SMEM)
    *branches, flags = pl.pallas_call(
        route_kernel,
        out_shape=[jax.ShapeDtypeStruct((1,), jnp.int32)] * (2 * micro_count)
        + [jax.ShapeDtypeStruct((2 * micro_count, width), jnp.int32)],
        in_specs=[smem],
        out_specs=[smem] * (2 * micro_count) + [pl.BlockSpec(memory_space=pltpu.VMEM)],
        scratch_shapes=[pltpu.SMEM((replicas,), jnp.int32)] * 3,
        compiler_params=pltpu.CompilerParams(vmem_limit_bytes=1 << 20),
    )(pair_order)
    branch = [number.reshape(()) for number in branches]
    flag = [flags[at : at + 1] == 0 for at in range(2 * micro_count)]
    return [(branch[2 * m : 2 * m + 2], flag[2 * m : 2 * m + 2]) for m in range(micro_count)]


def move_pairs(block, branch, pairs, beside, *given):
    def one(sigma, moved, *rest):
        if any(z != to for z, to in enumerate(sigma)):
            route = [(z * 4 + low, to * 4 + low) for z, to in enumerate(sigma) for low in range(4)]
            moved = lax.ppermute(moved, "rep", route)
        return moved, beside(*rest)

    every = [functools.partial(one, sigma) for sigma in itertools.permutations(range(pairs))]
    return lax.switch(branch, every, block, *given)


def swap(block, axis, bit):
    count = lax.axis_size(axis)
    return lax.ppermute(block, axis, [(i, i ^ bit) for i in range(count)])


def difference(own, other):
    spread = own.astype(jnp.float32) - other.astype(jnp.float32)
    return (distill_weight * spread).astype(jnp.bfloat16)


def sum_over(block, axis):
    if lax.axis_size(axis) == 2:
        return block + swap(block, axis, 1)
    return lax.psum(block, axis)


def after(block, *others):
    return lax.optimization_barrier((block, *others))[0]


def head_kernel(*refs):
    rows_ref, *blocks, out_ref, whole, sums, in_sem, out_sem = refs
    height = blocks[0].shape[0]
    arriving = [
        pltpu.make_async_copy(block, whole.at[pl.ds(at * height, height)], in_sem.at[at])
        for at, block in enumerate(blocks)
    ]
    for copy in arriving:
        copy.start()
    for copy in arriving:
        copy.wait()
    step = whole.shape[1] // head_parts
    leaving = []
    for part in range(head_parts):
        columns = pl.ds(part * step, step)
        sums[:, columns] = lax.dot_general(
            rows_ref[...],
            whole[:, columns],
            (((0,), (0,)), ((), ())),
            preferred_element_type=jnp.float32,
        ).astype(sums.dtype)
        copy = pltpu.make_async_copy(sums.at[:, columns], out_ref.at[:, columns], out_sem.at[part])
        copy.start()
        leaving.append(copy)
    for copy in leaving:
        copy.wait()


def head_gradient(rows, blocks):
    count, width = rows.shape
    vocab = blocks[0].shape[1]
    anywhere = pl.BlockSpec(memory_space=pl.ANY)
    return pl.pallas_call(
        head_kernel,
        out_shape=jax.ShapeDtypeStruct((width, vocab), jnp.bfloat16),
        in_specs=[pl.BlockSpec(memory_space=pltpu.VMEM)] + [anywhere] * len(blocks),
        out_specs=anywhere,
        scratch_shapes=[
            pltpu.VMEM((count, vocab), jnp.bfloat16),
            pltpu.VMEM((width, vocab), jnp.bfloat16),
            pltpu.SemaphoreType.DMA((len(blocks),)),
            pltpu.SemaphoreType.DMA((head_parts,)),
        ],
        compiler_params=pltpu.CompilerParams(vmem_limit_bytes=24 << 20),
        cost_estimate=pl.CostEstimate(
            flops=2 * count * width * vocab,
            bytes_accessed=2 * (count * width + count * vocab + width * vocab),
            transcendentals=0,
        ),
    )(rows, *blocks)


def after(block, *others):
    return lax.optimization_barrier((block, *others))[0]


def head_kernel(*refs):
    rows_ref, *blocks, out_ref, whole = refs
    height = blocks[0].shape[0]
    for at, block in enumerate(blocks):
        whole[pl.ds(at * height, height), :] = block[...]
    out_ref[...] = lax.dot_general(
        rows_ref[...], whole[...], (((0,), (0,)), ((), ())), preferred_element_type=jnp.float32
    ).astype(out_ref.dtype)


def head_gradient(rows, blocks):
    count, width = rows.shape
    vocab = blocks[0].shape[1]
    return pl.pallas_call(
        head_kernel,
        out_shape=jax.ShapeDtypeStruct((width, vocab), jnp.bfloat16),
        scratch_shapes=[pltpu.VMEM((count, vocab), jnp.bfloat16)],
        compiler_params=pltpu.CompilerParams(vmem_limit_bytes=24 << 20),
        cost_estimate=pl.CostEstimate(
            flops=2 * count * width * vocab,
            bytes_accessed=2 * (count * width + count * vocab + width * vocab),
            transcendentals=0,
        ),
    )(rows, *blocks)


def after(block, *others):
    return lax.optimization_barrier((block, *others))[0]


def head_kernel(*refs):
    rows_ref, *blocks, out_ref, whole = refs
    height = blocks[0].shape[0]
    for at, block in enumerate(blocks):
        whole[pl.ds(at * height, height), :] = block[...]
    out_ref[...] = lax.dot_general(
        rows_ref[...], whole[...], (((0,), (0,)), ((), ())), preferred_element_type=jnp.float32
    ).astype(out_ref.dtype)


def head_gradient(rows, blocks):
    count, width = rows.shape
    height, vocab = blocks[0].shape
    step = vocab // 4
    return pl.pallas_call(
        head_kernel,
        grid=(vocab // step,),
        out_shape=jax.ShapeDtypeStruct((width, vocab), jnp.bfloat16),
        in_specs=[pl.BlockSpec((count, width), lambda i: (0, 0))]
        + [pl.BlockSpec((height, step), lambda i: (0, i))] * len(blocks),
        out_specs=pl.BlockSpec((width, step), lambda i: (0, i)),
        scratch_shapes=[pltpu.VMEM((count, step), jnp.bfloat16)],
        compiler_params=pltpu.CompilerParams(vmem_limit_bytes=16 << 20),
        cost_estimate=pl.CostEstimate(
            flops=2 * count * width * vocab,
            bytes_accessed=2 * (count * width + count * vocab + width * vocab),
            transcendentals=0,
        ),
    )(rows, *blocks)


def paired_body(states, head_weight, pair_order, row_example):
    micro_count, row_count, half_width = states.shape
    place = lax.axis_index("rep")
    replica, side = place // 2, place % 2
    parity = replica % 2
    pairs = pair_order.shape[1] // 2
    quarter = row_count // 4
    local = jnp.arange(row_count, dtype=jnp.int32)
    block = local // quarter
    by_core = (block >> 1, block & 1)
    by_chip = (block & 1, block >> 1)
    examples = lax.dynamic_index_in_dim(row_example, replica, 1, keepdims=False)

    def onehots(order):
        other_core, other_chip = order
        example_of = (
            (side ^ other_core) * (2 * quarter) + (parity ^ other_chip) * quarter + local % quarter
        )
        return (examples[:, None, :] == example_of[None, :, None]).astype(jnp.bfloat16)

    onehot_core, onehot_chip = onehots(by_core), onehots(by_chip)

    logits = []
    for m in range(micro_count):
        rows = jnp.dot(onehot_core[m], states[m], preferred_element_type=jnp.float32)
        rows = rows.astype(jnp.bfloat16)
        theirs = jnp.dot(rows[2 * quarter :], head_weight, preferred_element_type=jnp.float32)
        arrived = swap(theirs, "rep", 1)
        own = jnp.dot(rows[: 2 * quarter], head_weight, preferred_element_type=jnp.float32)
        far = (own[quarter:] + arrived[quarter:]).astype(jnp.bfloat16)
        home = (own[:quarter] + arrived[:quarter]).astype(jnp.bfloat16)
        logits.append((home, far))
    sib = swap(logits[0][1], "rep", 2)
    codes = routes(after(pair_order, *logits[-1]), head_weight.shape[1])
    chip_rows = jnp.einsum(
        "mei,miw->mew", onehot_chip, after(states, *logits[0]), preferred_element_type=jnp.float32
    )
    chip_rows = chip_rows.astype(jnp.bfloat16)

    def settle(home, sib, first, second, to_home_first):
        grad_home = difference(home, jnp.where(to_home_first, first, second))
        grad_sib = difference(sib, jnp.where(to_home_first, second, first))
        return grad_home, grad_sib

    def leaving(home, sib, home_first):
        return jnp.where(home_first, home, sib), jnp.where(home_first, sib, home)

    def partial_state(*blocks):
        gradient = jnp.concatenate(blocks, axis=0)
        partial = jnp.einsum(
            "rv,wv->rw", gradient, head_weight, preferred_element_type=jnp.float32
        )
        return partial, partial.astype(jnp.bfloat16)

    def whole_state(partial, sent, *before):
        other = after(swap(sent, "voc", 1), *before).astype(jnp.float32)
        return (partial + other).astype(jnp.bfloat16)

    def beside(nexts, settled):
        arriving = [swap(far, "rep", 2) for far in nexts]
        return arriving, [swap(grad_sib, "rep", 2) for _, grad_sib in settled]

    def second_beside(returned):
        return [(swap(home, "rep", 1), swap(far, "rep", 1)) for home, far in returned]

    early, settled = [], []
    for m in range(micro_count):
        home = logits[m][0]
        branches, (home_first, to_home_first) = codes[m]
        sent = leaving(home, sib, home_first)
        nexts = [] if m + 1 == micro_count else [logits[m + 1][1]]
        if m == 0:
            sent = [after(block, chip_rows) for block in sent]
        else:
            sent = [after(block, *settled[0]) for block in sent]
        first, (arriving, returned) = move_pairs(
            sent[0], branches[0], pairs, beside, nexts, settled
        )
        returned = [(group[0], far) for group, far in zip(settled, returned)]
        second, swapped = move_pairs(
            after(sent[1], first), branches[1], pairs, second_beside, returned
        )
        for (grad_home, far), (near, farther) in zip(returned, swapped):
            early.append((grad_home, near, far, farther))
        settled = [settle(home, sib, first, second, to_home_first)]
        sib = arriving[0] if arriving else None
    [(grad_home, grad_sib)] = settled
    far = swap(grad_sib, "rep", 2)
    near = swap(grad_home, "rep", 1)
    early = [[after(block, near) for block in group] for group in early]
    parts = [partial_state(*group) for group in [*early, (grad_home, near)]]
    far = after(far, *[sent for _, sent in parts])
    farther = swap(far, "rep", 1)
    head_grad = head_gradient(
        chip_rows.reshape(micro_count * row_count, half_width),
        sum(early, []) + [grad_home, near, far, farther],
    )
    canon = [whole_state(*part, head_grad) for part in parts[:-1]]
    last = [whole_state(*parts[-1]), whole_state(*partial_state(far, farther))]
    canon.append(jnp.concatenate(last, axis=0))
    state_grad = jnp.einsum(
        "mei,mew->miw", onehot_chip, jnp.stack(canon), preferred_element_type=jnp.float32
    ).astype(jnp.bfloat16)
    return state_grad, head_grad


def spread_body(states, head_weight, pair_order, row_example):
    micro_count, row_count, half_width = states.shape
    devices = lax.axis_size("rep")
    place = lax.axis_index("rep")
    replica, side = place // 2, place % 2
    half = row_count // 2
    local = jnp.arange(row_count, dtype=jnp.int32)
    example_of = (side ^ (local // half)) * half + local % half
    examples = lax.dynamic_index_in_dim(row_example, replica, 1, keepdims=False)
    onehot = (examples[:, None, :] == example_of[None, :, None]).astype(jnp.bfloat16)
    ordered = jnp.einsum("mei,miw->mew", onehot, states, preferred_element_type=jnp.float32)
    ordered = ordered.astype(jnp.bfloat16)
    partner = partner_table(pair_order)
    sources = jnp.arange(devices, dtype=jnp.int32)
    partner_dev = 2 * jnp.repeat(partner, 2, axis=1) + sources % 2
    state_parts, gradients = [], []
    for m in range(micro_count):
        partial = jnp.dot(ordered[m], head_weight, preferred_element_type=jnp.float32)
        logits = (partial[:half] + swap(partial[half:], "rep", 1)).astype(jnp.bfloat16)
        tiles = logits.reshape(devices, half // devices, -1)
        tiles = lax.all_to_all(tiles, "rep", split_axis=0, concat_axis=0, tiled=True)
        mates = (partner_dev[m][:, None] == sources[None, :]).astype(jnp.bfloat16)
        mate_tiles = jnp.einsum("ds,srv->drv", mates, tiles, preferred_element_type=jnp.float32)
        graded = difference(tiles, mate_tiles)
        graded = lax.all_to_all(graded, "rep", split_axis=0, concat_axis=0, tiled=True)
        graded = graded.reshape(half, -1)
        gradient = jnp.concatenate([graded, swap(graded, "rep", 1)], axis=0)
        gradients.append(gradient)
        back = jnp.einsum("rv,wv->rw", gradient, head_weight, preferred_element_type=jnp.float32)
        state_canon = sum_over(back, "voc").astype(jnp.bfloat16)
        state_parts.append(
            jnp.einsum("ei,ew->iw", onehot[m], state_canon, preferred_element_type=jnp.float32)
        )
    state_grad = jnp.stack(state_parts).astype(jnp.bfloat16)
    head_grad = jnp.einsum(
        "mrw,mrv->wv", ordered, jnp.stack(gradients), preferred_element_type=jnp.float32
    )
    return state_grad, head_grad.astype(jnp.bfloat16)


def solution(mesh):
    replicas = mesh.shape["rep"] // 2
    few = replicas % 2 == 0 and math.factorial(replicas // 2) <= max_permutations
    few = few and mesh.shape["voc"] == 2
    return jax.shard_map(
        paired_body if few else spread_body,
        mesh=mesh,
        in_specs=(P(None, None, "rep"), P("rep", "voc"), P(), P()),
        out_specs=(P(None, None, "rep"), P("rep", "voc")),
        check_vma=False,
    )
```

profile of v0, /device:TPU:0, one launch (start us, length us, event | category | flops | bytes accessed | tf_op | source)
XLA Modules:
  0.0 79.4 jit_solution(9845294189092606440)
XLA Ops:
  0.7 0.8 %constant_dynamic-slice_fusion = s32[2,1,256]{2,1,0:T(1,128)S(1)} fusion(s32[2,8,256]{2,1,0:T(8,128)} %param.103, s32[]{:T(128)S(6)} %select_n.80), kind=kLoop, calls=%fused_computation.79 | loop fusion | bytes 4100 | tf_op jit(solution)/shard_map/jit(dynamic_index_in_dim)/dynamic_slice | solution.py:235
  1.7 1.3 %convolution_convert_fusion.3 = bf16[256,384]{1,0:T(8,128)(2,1)S(1)} fusion(pred[2,256,256]{1,2,0:T(32,128)(4,1)S(1)} %broadcast_compare_fusion, bf16[2,256,384]{2,1,0:T(8,128)(2,1)} %param.100), kind=kOutput, calls=%fused_computation.3 | convolution fusion | flops 50429952 | bytes 458752 | tf_op jit(solution)/shard_map/dot_general | solution.py:248
  6.3 3.0 %collective-permute-start.190 = (bf16[64,2048]{1,0:T(8,128)(2,1)S(1)}, bf16[64,2048]{1,0:T(8,128)(2,1)S(1)}, u32[]{:S(2)}, u32[]{:S(2)}) collective-permute-start(bf16[64,2048]{1,0:T(8,128)(2,1)S(1)} %fusion.10), channel_id=1, source_target_pairs={{0,4},{2,6},{4,0},{6,2},{8,12},{10,14},{12,8},{14,10},{16,20},{18,... | collective-permute-start | bytes 786440 | tf_op jit(solution)/shard_map/ppermute | solution.py:89
  9.4 1.4 %shard_map.59 = (s32[1]{0:T(128)}, s32[1]{0:T(128)}, s32[1]{0:T(128)}, s32[1]{0:T(128)}, s32[4,2048]{1,0:T(4,128)S(1)}) custom-call(s32[2,8]{1,0:T(2,128)S(1)} %copy-done.1), custom_call_target="tpu_custom_call" | custom-call | tf_op jit(solution)/shard_map/pallas_call | solution.py:62
  13.5 2.4 %collective-permute-done.190 = bf16[64,2048]{1,0:T(8,128)(2,1)S(1)} collective-permute-done((bf16[64,2048]{1,0:T(8,128)(2,1)S(1)}, bf16[64,2048]{1,0:T(8,128)(2,1)S(1)}, u32[]{:S(2)}, u32[]{:S(2)}) %collective-permute-start.190) | collective-permute-done | bytes 262176 | tf_op jit(solution)/shard_map/ppermute | solution.py:89
  16.4 9.2 %conditional.4 = (bf16[64,2048]{1,0:T(8,128)(2,1)S(1)}, bf16[64,2048]{1,0:T(8,128)(2,1)}) conditional(s32[]{:T(128)} %bitcast.4, (bf16[64,2048]{1,0:T(8,128)(2,1)S(1)}, bf16[64,2048]{1,0:T(8,128)(2,1)S(1)}) %tuple.385, (bf16[64,2048]{1,0:T(8,128)(2,1)S(1)}, bf16[64,2048]{1,0:T(8,128)(2,1)S(1)}) %tuple.386, ...), branch_computations={%region_0.1_spmd, %region_1.2_spmd, %region_2.3_spmd, %region_3.4_... | conditional | bytes 2621536 | solution.py:84
  16.5 1.8 %collective-permute-start.19 = (bf16[64,2048]{1,0:T(8,128)(2,1)S(1)}, bf16[64,2048]{1,0:T(8,128)(2,1)S(1)}, u32[]{:S(2)}, u32[]{:S(2)}) collective-permute-start(bf16[64,2048]{1,0:T(8,128)(2,1)S(1)} %get-tuple-element.405), channel_id=1, source_target_pairs={{0,8},{2,10},{4,12},{6,14},{8,24},{10,26},{12,28},{14,30},{16,0},{... | collective-permute-start | bytes 786440 | tf_op jit(solution)/shard_map/cond/branch_10_fun/ppermute | solution.py:80
  18.3 1.5 %collective-permute-start.20 = (bf16[64,2048]{1,0:T(8,128)(2,1)S(1)}, bf16[64,2048]{1,0:T(8,128)(2,1)}, u32[]{:S(2)}, u32[]{:S(2)}) collective-permute-start(bf16[64,2048]{1,0:T(8,128)(2,1)S(1)} %get-tuple-element.406), channel_id=1, source_target_pairs={{0,4},{2,6},{4,0},{6,2},{8,12},{10,14},{12,8},{14,10},{16,20},{18,... | collective-permute-start | bytes 786440 | tf_op jit(solution)/shard_map/cond/branch_10_fun/ppermute | solution.py:89
  19.9 5.4 %collective-permute-done.19 = bf16[64,2048]{1,0:T(8,128)(2,1)S(1)} collective-permute-done((bf16[64,2048]{1,0:T(8,128)(2,1)S(1)}, bf16[64,2048]{1,0:T(8,128)(2,1)S(1)}, u32[]{:S(2)}, u32[]{:S(2)}) %collective-permute-start.19) | collective-permute-done | bytes 262176 | tf_op jit(solution)/shard_map/cond/branch_10_fun/ppermute | solution.py:80
  25.7 13.2 %conditional.5 = (bf16[64,2048]{1,0:T(8,128)(2,1)S(1)}) conditional(s32[]{:T(128)} %bitcast.5, bf16[64,2048]{1,0:T(8,128)(2,1)S(1)} %get-tuple-element.589, bf16[64,2048]{1,0:T(8,128)(2,1)S(1)} %get-tuple-element.589, bf16[64,2048]{1,0:T(8,128)(2,1)S(1)} %get-tuple-element.589, ...), branch_computations={%region_24.25_spmd, %region_25.26_spmd, %region_26.27_spmd, %regio... | conditional | bytes 1572912 | solution.py:84
  25.7 3.3 %collective-permute-start.68 = (bf16[64,2048]{1,0:T(8,128)(2,1)S(1)}, bf16[64,2048]{1,0:T(8,128)(2,1)S(1)}, u32[]{:S(2)}, u32[]{:S(2)}) collective-permute-start(bf16[64,2048]{1,0:T(8,128)(2,1)S(1)} %param.46), channel_id=1, source_target_pairs={{0,24},{2,26},{4,28},{6,30},{8,16},{10,18},{12,20},{14,22},{16,0},... | collective-permute-start | bytes 786440 | tf_op jit(solution)/shard_map/cond/branch_22_fun/ppermute | solution.py:80
  29.0 9.9 %collective-permute-done.68 = bf16[64,2048]{1,0:T(8,128)(2,1)S(1)} collective-permute-done((bf16[64,2048]{1,0:T(8,128)(2,1)S(1)}, bf16[64,2048]{1,0:T(8,128)(2,1)S(1)}, u32[]{:S(2)}, u32[]{:S(2)}) %collective-permute-start.68) | collective-permute-done | bytes 262176 | tf_op jit(solution)/shard_map/cond/branch_22_fun/ppermute | solution.py:80
  38.9 1.1 %broadcast_select_fusion = (bf16[64,2048]{1,0:T(8,128)(2,1)S(1)}, bf16[64,2048]{1,0:T(8,128)(2,1)S(1)}) fusion(bf16[64,2048]{1,0:T(8,128)(2,1)} %get-tuple-element.591, bf16[64,2048]{1,0:T(8,128)(2,1)S(1)} %get-tuple-element.614, pred[2048]{0:T(1024)(128)(4,1)S(1)} %get-tuple-element.608), kind=kLoop, calls=%fused_computation.45 | loop fusion | flops 262144 | bytes 1050624 | tf_op jit(solution)/shard_map/jit(_where)/select_n | solution.py:269
  40.0 1.2 %multiply_convert_fusion.2 = (bf16[64,2048]{1,0:T(8,128)(2,1)S(1)}, bf16[64,2048]{1,0:T(8,128)(2,1)S(1)}) fusion(bf16[64,2048]{1,0:T(8,128)(2,1)S(1)} %collective-permute-done.190, bf16[64,2048]{1,0:T(8,128)(2,1)} %copy-done.2, bf16[64,2048]{1,0:T(8,128)(2,1)S(1)} %get-tuple-element.586, pred[2048]{0:T(1024)(128)(4,1)S(1)} %get-tuple-element.610, ...), kind=kLoop, calls=%fused_computation.32 | loop fusion | flops 1572864 | bytes 1574912 | tf_op jit(solution)/shard_map/convert_element_type | solution.py:94
  41.2 8.6 %conditional.6 = (bf16[64,2048]{1,0:T(8,128)(2,1)S(1)}, bf16[64,2048]{1,0:T(8,128)(2,1)}) conditional(s32[]{:T(128)} %bitcast.6, (bf16[64,2048]{1,0:T(8,128)(2,1)S(1)}, bf16[64,2048]{1,0:T(8,128)(2,1)S(1)}) %tuple.390, (bf16[64,2048]{1,0:T(8,128)(2,1)S(1)}, bf16[64,2048]{1,0:T(8,128)(2,1)S(1)}) %tuple.391, ...), branch_computations={%region_48.49_spmd, %region_49.50_spmd, %region_50.51_spmd, %regio... | conditional | bytes 2621536 | solution.py:84
  41.3 1.2 %collective-permute-start.88 = (bf16[64,2048]{1,0:T(8,128)(2,1)S(1)}, bf16[64,2048]{1,0:T(8,128)(2,1)}, u32[]{:S(2)}, u32[]{:S(2)}) collective-permute-start(bf16[64,2048]{1,0:T(8,128)(2,1)S(1)} %get-tuple-element.452), channel_id=1, source_target_pairs={{0,4},{2,6},{4,0},{6,2},{8,12},{10,14},{12,8},{14,10},{16,20},{18,... | collective-permute-start | bytes 786440 | tf_op jit(solution)/shard_map/cond/branch_9_fun/ppermute | solution.py:89
  42.5 7.0 %collective-permute-done.87 = bf16[64,2048]{1,0:T(8,128)(2,1)S(1)} collective-permute-done((bf16[64,2048]{1,0:T(8,128)(2,1)S(1)}, bf16[64,2048]{1,0:T(8,128)(2,1)S(1)}, u32[]{:S(2)}, u32[]{:S(2)}) %collective-permute-start.87) | collective-permute-done | bytes 262176 | tf_op jit(solution)/shard_map/cond/branch_9_fun/ppermute | solution.py:80
  49.8 0.7 copy-done.3
  50.5 8.3 %conditional.7 = (bf16[64,2048]{1,0:T(8,128)(2,1)S(1)}, bf16[64,2048]{1,0:T(8,128)(2,1)}, bf16[64,2048]{1,0:T(8,128)(2,1)}) conditional(s32[]{:T(128)} %bitcast.7, (bf16[64,2048]{1,0:T(8,128)(2,1)S(1)}, bf16[64,2048]{1,0:T(8,128)(2,1)}, bf16[64,2048]{1,0:T(8,128)(2,1)S(1)}) %tuple.394, ...), branch_computations={%region_72.73_spmd, %region_73.74_spmd, %region_74.75_spmd, %regio... | conditional | bytes 3670160 | solution.py:84
  50.5 3.7 %collective-permute-start.173 = (bf16[64,2048]{1,0:T(8,128)(2,1)S(1)}, bf16[64,2048]{1,0:T(8,128)(2,1)S(1)}, u32[]{:S(2)}, u32[]{:S(2)}) collective-permute-start(bf16[64,2048]{1,0:T(8,128)(2,1)S(1)} %get-tuple-element.538), channel_id=1, source_target_pairs={{0,24},{2,26},{4,28},{6,30},{8,0},{10,2},{12,4},{14,6},{16,16},{18... | collective-permute-start | bytes 786440 | tf_op jit(solution)/shard_map/cond/branch_19_fun/ppermute | solution.py:80
  54.8 4.0 %collective-permute-done.173 = bf16[64,2048]{1,0:T(8,128)(2,1)S(1)} collective-permute-done((bf16[64,2048]{1,0:T(8,128)(2,1)S(1)}, bf16[64,2048]{1,0:T(8,128)(2,1)S(1)}, u32[]{:S(2)}, u32[]{:S(2)}) %collective-permute-start.173) | collective-permute-done | bytes 262176 | tf_op jit(solution)/shard_map/cond/branch_19_fun/ppermute | solution.py:80
  58.8 1.2 %multiply_convert_fusion.1 = (bf16[64,2048]{1,0:T(8,128)(2,1)S(1)}, bf16[64,2048]{1,0:T(8,128)(2,1)S(1)}) fusion(bf16[64,2048]{1,0:T(8,128)(2,1)S(1)} %get-tuple-element.614, bf16[64,2048]{1,0:T(8,128)(2,1)} %copy-done.3, bf16[64,2048]{1,0:T(8,128)(2,1)S(1)} %get-tuple-element.598, pred[2048]{0:T(1024)(128)(4,1)S(1)} %get-tuple-element.607, ...), kind=kLoop, calls=%fused_computation.31 | loop fusion | flops 1572864 | bytes 1574912 | tf_op jit(solution)/shard_map/convert_element_type | solution.py:94
  60.1 1.1 %collective-permute-start.193 = (bf16[64,2048]{1,0:T(8,128)(2,1)S(1)}, bf16[64,2048]{1,0:T(8,128)(2,1)S(1)}, u32[]{:S(2)}, u32[]{:S(2)}) collective-permute-start(bf16[64,2048]{1,0:T(8,128)(2,1)S(1)} %get-tuple-element.616), channel_id=1, source_target_pairs={{0,4},{2,6},{4,0},{6,2},{8,12},{10,14},{12,8},{14,10},{16,20},{18,... | collective-permute-start | bytes 786440 | tf_op jit(solution)/shard_map/ppermute | solution.py:89
  61.7 0.6 fusion.50
  62.3 1.2 %collective-permute-start.195 = (bf16[128,384]{1,0:T(8,128)(2,1)S(1)}, bf16[128,384]{1,0:T(8,128)(2,1)S(1)}, u32[]{:S(2)}, u32[]{:S(2)}) collective-permute-start(bf16[128,384]{1,0:T(8,128)(2,1)S(1)} %get-tuple-element.623), channel_id=1, source_target_pairs={{0,1},{1,0},{2,3},{3,2},{4,5},{5,4},{6,7},{7,6},{8,9},{9,8},{10,11... | collective-permute-start | bytes 294920 | tf_op jit(solution)/shard_map/ppermute | solution.py:89
  63.4 1.8 %fusion.49 = (bf16[256,384]{1,0:T(8,128)(2,1)S(1)}, f32[256,384]{1,0:T(8,128)S(1)}) fusion(bf16[384,2048]{1,0:T(8,128)(2,1)S(1)} %copy-done, bf16[64,2048]{1,0:T(8,128)(2,1)} %get-tuple-element.604.refs_4_, bf16[64,2048]{1,0:T(8,128)(2,1)} %get-tuple-element.602.refs_3_, bf16[64,2048]{1,0:T(8,128)(2,1)} %get-tuple-element.601.refs_2_, ...), kind=kOutput, calls=%fused_computation.84 | convolution fusion | flops 406945792 | bytes 3211264 | tf_op jit(solution)/shard_map/rv,wv->rw/dot_general | solution.py:273
  65.2 3.6 %collective-permute-done.193.refs_7_ = bf16[64,2048]{1,0:T(8,128)(2,1)S(1)} collective-permute-done((bf16[64,2048]{1,0:T(8,128)(2,1)S(1)}, bf16[64,2048]{1,0:T(8,128)(2,1)S(1)}, u32[]{:S(2)}, u32[]{:S(2)}) %collective-permute-start.193) | collective-permute-done | bytes 262176 | tf_op jit(solution)/shard_map/ppermute | solution.py:89
  68.9 1.0 %collective-permute-start.192 = (bf16[256,384]{1,0:T(8,128)(2,1)S(1)}, bf16[256,384]{1,0:T(8,128)(2,1)S(1)}, u32[]{:S(2)}, u32[]{:S(2)}) collective-permute-start(bf16[256,384]{1,0:T(8,128)(2,1)S(1)} %get-tuple-element.621), channel_id=1, source_target_pairs={{0,1},{1,0},{2,3},{3,2},{4,5},{5,4},{6,7},{7,6},{8,9},{9,8},{10,11... | collective-permute-start | bytes 589832 | tf_op jit(solution)/shard_map/ppermute | solution.py:89
  71.0 1.1 %collective-permute-start.196 = (bf16[128,384]{1,0:T(8,128)(2,1)S(1)}, bf16[128,384]{1,0:T(8,128)(2,1)S(1)}, u32[]{:S(2)}, u32[]{:S(2)}) collective-permute-start(bf16[128,384]{1,0:T(8,128)(2,1)S(1)} %get-tuple-element.625), channel_id=1, source_target_pairs={{0,1},{1,0},{2,3},{3,2},{4,5},{5,4},{6,7},{7,6},{8,9},{9,8},{10,11... | collective-permute-start | bytes 294920 | tf_op jit(solution)/shard_map/ppermute | solution.py:89
  72.1 4.1 %shard_map.60 = bf16[384,2048]{1,0:T(8,128)(2,1)} custom-call(bf16[512,384]{1,0:T(8,128)(2,1)S(1)} %bitcast.32, bf16[64,2048]{1,0:T(8,128)(2,1)S(1)} %get-tuple-element.599.refs_1_, bf16[64,2048]{1,0:T(8,128)(2,1)} %get-tuple-element.601.refs_2_, bf16[64,2048]{1,0:T(8,128)(2,1)} %get-tuple-element.602.refs_3_, bf16[64,2048]{1,0:T(8,128)(2,1)} %get-tuple-element.604.refs_4_, ...), custom_call_target="tpu_custom_call" | custom-call | flops 805306368 | bytes 4063232 | tf_op jit(solution)/shard_map/pallas_call | solution.py:207
  76.6 1.7 %collective-permute-done.196 = bf16[128,384]{1,0:T(8,128)(2,1)S(1)} collective-permute-done((bf16[128,384]{1,0:T(8,128)(2,1)S(1)}, bf16[128,384]{1,0:T(8,128)(2,1)S(1)}, u32[]{:S(2)}, u32[]{:S(2)}) %collective-permute-start.196) | collective-permute-done | bytes 98336 | tf_op jit(solution)/shard_map/ppermute | solution.py:89
  78.3 1.1 %convolution_convert_fusion = bf16[2,256,384]{2,1,0:T(8,128)(2,1)} fusion(bf16[1,256,384]{2,1,0:T(8,128)(2,1)S(1)} %maximum_bitcast_fusion, bf16[1,256,384]{2,1,0:T(8,128)(2,1)S(1)} %fusion.29, s32[256]{0:T(256)S(1)} %copy-done.6, s32[2,256]{1,0:T(2,128)S(1)} %bitcast.35), kind=kOutput, calls=%fused_computation | convolution fusion | flops 101187584 | bytes 789504 | tf_op jit(solution)/shard_map/mei,mew->miw/dot_general | solution.py:324
  (54 shorter events, 7.3 us)
Async XLA Ops:
  0.6 2.3 %copy-start = (bf16[384,2048]{1,0:T(8,128)(2,1)S(1)}, bf16[384,2048]{1,0:T(8,128)(2,1)}, u32[]{:S(2)}) copy-start(bf16[384,2048]{1,0:T(8,128)(2,1)} %param.101) | copy-start | bytes 4718596
  1.7 2.3 %copy-start.4 = (bf16[2,256,384]{2,1,0:T(8,128)(2,1)S(1)}, bf16[2,256,384]{2,1,0:T(8,128)(2,1)}, u32[]{:S(2)}) copy-start(bf16[2,256,384]{2,1,0:T(8,128)(2,1)} %param.100) | copy-start | bytes 1179652
  3.4 2.8 %collective-permute-start.188 = (f32[128,2048]{1,0:T(8,128)S(1)}, f32[128,2048]{1,0:T(8,128)S(1)}, u32[]{:S(2)}, u32[]{:S(2)}) collective-permute-start(f32[128,2048]{1,0:T(8,128)S(1)} %fusion.38), channel_id=1, source_target_pairs={{0,2},{2,0},{4,6},{6,4},{8,10},{10,8},{12,14},{14,12},{16,18},{18,... | collective-permute-start | bytes 3145736 | tf_op jit(solution)/shard_map/ppermute | solution.py:89
  4.7 4.6 %collective-permute-start.189 = (f32[128,2048]{1,0:T(8,128)S(1)}, f32[128,2048]{1,0:T(8,128)S(1)}, u32[]{:S(2)}, u32[]{:S(2)}) collective-permute-start(f32[128,2048]{1,0:T(8,128)S(1)} %fusion.34), channel_id=1, source_target_pairs={{0,2},{2,0},{4,6},{6,4},{8,10},{10,8},{12,14},{14,12},{16,18},{18,... | collective-permute-start | bytes 3145736 | tf_op jit(solution)/shard_map/ppermute | solution.py:89
  4.8 11.2 %copy-start.5 = (s32[256]{0:T(256)}, s32[256]{0:T(256)S(1)}, u32[]{:S(2)}) copy-start(s32[256]{0:T(256)S(1)} %add_add_fusion.1) | copy-start | bytes 3076
  6.3 3.1 %copy-start.1 = (s32[2,8]{1,0:T(2,128)S(1)}, s32[2,8]{1,0:T(2,128)}, u32[]{:S(2)}) copy-start(s32[2,8]{1,0:T(2,128)} %order_ref) | copy-start | bytes 196
  6.3 9.6 %collective-permute-start.190 = (bf16[64,2048]{1,0:T(8,128)(2,1)S(1)}, bf16[64,2048]{1,0:T(8,128)(2,1)S(1)}, u32[]{:S(2)}, u32[]{:S(2)}) collective-permute-start(bf16[64,2048]{1,0:T(8,128)(2,1)S(1)} %fusion.10), channel_id=1, source_target_pairs={{0,4},{2,6},{4,0},{6,2},{8,12},{10,14},{12,8},{14,10},{16,20},{18,... | collective-permute-start | bytes 786440 | tf_op jit(solution)/shard_map/ppermute | solution.py:89
  16.5 8.8 %collective-permute-start.19 = (bf16[64,2048]{1,0:T(8,128)(2,1)S(1)}, bf16[64,2048]{1,0:T(8,128)(2,1)S(1)}, u32[]{:S(2)}, u32[]{:S(2)}) collective-permute-start(bf16[64,2048]{1,0:T(8,128)(2,1)S(1)} %get-tuple-element.405), channel_id=1, source_target_pairs={{0,8},{2,10},{4,12},{6,14},{8,24},{10,26},{12,28},{14,30},{16,0},{... | collective-permute-start | bytes 786440 | tf_op jit(solution)/shard_map/cond/branch_10_fun/ppermute | solution.py:80
  18.3 7.3 %collective-permute-start.20 = (bf16[64,2048]{1,0:T(8,128)(2,1)S(1)}, bf16[64,2048]{1,0:T(8,128)(2,1)}, u32[]{:S(2)}, u32[]{:S(2)}) collective-permute-start(bf16[64,2048]{1,0:T(8,128)(2,1)S(1)} %get-tuple-element.406), channel_id=1, source_target_pairs={{0,4},{2,6},{4,0},{6,2},{8,12},{10,14},{12,8},{14,10},{16,20},{18,... | collective-permute-start | bytes 786440 | tf_op jit(solution)/shard_map/cond/branch_10_fun/ppermute | solution.py:89
  25.7 13.2 %collective-permute-start.68 = (bf16[64,2048]{1,0:T(8,128)(2,1)S(1)}, bf16[64,2048]{1,0:T(8,128)(2,1)S(1)}, u32[]{:S(2)}, u32[]{:S(2)}) collective-permute-start(bf16[64,2048]{1,0:T(8,128)(2,1)S(1)} %param.46), channel_id=1, source_target_pairs={{0,24},{2,26},{4,28},{6,30},{8,16},{10,18},{12,20},{14,22},{16,0},... | collective-permute-start | bytes 786440 | tf_op jit(solution)/shard_map/cond/branch_22_fun/ppermute | solution.py:80
  38.9 1.1 %copy-start.2 = (bf16[64,2048]{1,0:T(8,128)(2,1)}, bf16[64,2048]{1,0:T(8,128)(2,1)S(1)}, u32[]{:S(2)}) copy-start(bf16[64,2048]{1,0:T(8,128)(2,1)S(1)} %get-tuple-element.795) | copy-start | bytes 786436
  41.2 8.3 %collective-permute-start.87 = (bf16[64,2048]{1,0:T(8,128)(2,1)S(1)}, bf16[64,2048]{1,0:T(8,128)(2,1)S(1)}, u32[]{:S(2)}, u32[]{:S(2)}) collective-permute-start(bf16[64,2048]{1,0:T(8,128)(2,1)S(1)} %get-tuple-element.451), channel_id=1, source_target_pairs={{0,8},{2,10},{4,12},{6,14},{8,16},{10,18},{12,20},{14,22},{16,24},... | collective-permute-start | bytes 786440 | tf_op jit(solution)/shard_map/cond/branch_9_fun/ppermute | solution.py:80
  41.3 8.3 %collective-permute-start.88 = (bf16[64,2048]{1,0:T(8,128)(2,1)S(1)}, bf16[64,2048]{1,0:T(8,128)(2,1)}, u32[]{:S(2)}, u32[]{:S(2)}) collective-permute-start(bf16[64,2048]{1,0:T(8,128)(2,1)S(1)} %get-tuple-element.452), channel_id=1, source_target_pairs={{0,4},{2,6},{4,0},{6,2},{8,12},{10,14},{12,8},{14,10},{16,20},{18,... | collective-permute-start | bytes 786440 | tf_op jit(solution)/shard_map/cond/branch_9_fun/ppermute | solution.py:89
  49.8 0.7 copy-start.3
  50.5 8.3 %collective-permute-start.173 = (bf16[64,2048]{1,0:T(8,128)(2,1)S(1)}, bf16[64,2048]{1,0:T(8,128)(2,1)S(1)}, u32[]{:S(2)}, u32[]{:S(2)}) collective-permute-start(bf16[64,2048]{1,0:T(8,128)(2,1)S(1)} %get-tuple-element.538), channel_id=1, source_target_pairs={{0,24},{2,26},{4,28},{6,30},{8,0},{10,2},{12,4},{14,6},{16,16},{18... | collective-permute-start | bytes 786440 | tf_op jit(solution)/shard_map/cond/branch_19_fun/ppermute | solution.py:80
  54.2 4.6 %collective-permute-start.174 = (bf16[64,2048]{1,0:T(8,128)(2,1)S(1)}, bf16[64,2048]{1,0:T(8,128)(2,1)}, u32[]{:S(2)}, u32[]{:S(2)}) collective-permute-start(bf16[64,2048]{1,0:T(8,128)(2,1)S(1)} %get-tuple-element.539), channel_id=1, source_target_pairs={{0,2},{2,0},{4,6},{6,4},{8,10},{10,8},{12,14},{14,12},{16,18},{18,... | collective-permute-start | bytes 786440 | tf_op jit(solution)/shard_map/cond/branch_19_fun/ppermute | solution.py:89
  54.3 4.5 %collective-permute-start.175 = (bf16[64,2048]{1,0:T(8,128)(2,1)}, bf16[64,2048]{1,0:T(8,128)(2,1)}, u32[]{:S(2)}, u32[]{:S(2)}) collective-permute-start(bf16[64,2048]{1,0:T(8,128)(2,1)} %get-tuple-element.540), channel_id=1, source_target_pairs={{0,2},{2,0},{4,6},{6,4},{8,10},{10,8},{12,14},{14,12},{16,18},{18,... | collective-permute-start | bytes 786440 | tf_op jit(solution)/shard_map/cond/branch_19_fun/ppermute | solution.py:89
  60.1 1.6 %collective-permute-start.191 = (bf16[64,2048]{1,0:T(8,128)(2,1)S(1)}, bf16[64,2048]{1,0:T(8,128)(2,1)S(1)}, u32[]{:S(2)}, u32[]{:S(2)}) collective-permute-start(bf16[64,2048]{1,0:T(8,128)(2,1)S(1)} %get-tuple-element.615.refs_5_), channel_id=1, source_target_pairs={{0,2},{2,0},{4,6},{6,4},{8,10},{10,8},{12,14},{14,12},{16,18},{18,... | collective-permute-start | bytes 786440 | tf_op jit(solution)/shard_map/ppermute | solution.py:89
  60.1 8.7 %collective-permute-start.193 = (bf16[64,2048]{1,0:T(8,128)(2,1)S(1)}, bf16[64,2048]{1,0:T(8,128)(2,1)S(1)}, u32[]{:S(2)}, u32[]{:S(2)}) collective-permute-start(bf16[64,2048]{1,0:T(8,128)(2,1)S(1)} %get-tuple-element.616), channel_id=1, source_target_pairs={{0,4},{2,6},{4,0},{6,2},{8,12},{10,14},{12,8},{14,10},{16,20},{18,... | collective-permute-start | bytes 786440 | tf_op jit(solution)/shard_map/ppermute | solution.py:89
  62.3 7.6 %collective-permute-start.195 = (bf16[128,384]{1,0:T(8,128)(2,1)S(1)}, bf16[128,384]{1,0:T(8,128)(2,1)S(1)}, u32[]{:S(2)}, u32[]{:S(2)}) collective-permute-start(bf16[128,384]{1,0:T(8,128)(2,1)S(1)} %get-tuple-element.623), channel_id=1, source_target_pairs={{0,1},{1,0},{2,3},{3,2},{4,5},{5,4},{6,7},{7,6},{8,9},{9,8},{10,11... | collective-permute-start | bytes 294920 | tf_op jit(solution)/shard_map/ppermute | solution.py:89
  68.9 1.5 %collective-permute-start.194 = (bf16[64,2048]{1,0:T(8,128)(2,1)S(1)}, bf16[64,2048]{1,0:T(8,128)(2,1)S(1)}, u32[]{:S(2)}, u32[]{:S(2)}) collective-permute-start(bf16[64,2048]{1,0:T(8,128)(2,1)S(1)} %collective-permute-done.193.refs_7_), channel_id=1, source_target_pairs={{0,2},{2,0},{4,6},{6,4},{8,10},{10,8},{12,14},{14,12},{16,18},{18,... | collective-permute-start | bytes 786440 | tf_op jit(solution)/shard_map/ppermute | solution.py:89
  68.9 7.7 %collective-permute-start.192 = (bf16[256,384]{1,0:T(8,128)(2,1)S(1)}, bf16[256,384]{1,0:T(8,128)(2,1)S(1)}, u32[]{:S(2)}, u32[]{:S(2)}) collective-permute-start(bf16[256,384]{1,0:T(8,128)(2,1)S(1)} %get-tuple-element.621), channel_id=1, source_target_pairs={{0,1},{1,0},{2,3},{3,2},{4,5},{5,4},{6,7},{7,6},{8,9},{9,8},{10,11... | collective-permute-start | bytes 589832 | tf_op jit(solution)/shard_map/ppermute | solution.py:89
  71.0 7.3 %collective-permute-start.196 = (bf16[128,384]{1,0:T(8,128)(2,1)S(1)}, bf16[128,384]{1,0:T(8,128)(2,1)S(1)}, u32[]{:S(2)}, u32[]{:S(2)}) collective-permute-start(bf16[128,384]{1,0:T(8,128)(2,1)S(1)} %get-tuple-element.625), channel_id=1, source_target_pairs={{0,1},{1,0},{2,3},{3,2},{4,5},{5,4},{6,7},{7,6},{8,9},{9,8},{10,11... | collective-permute-start | bytes 294920 | tf_op jit(solution)/shard_map/ppermute | solution.py:89
  76.2 2.1 %copy-start.6 = (s32[256]{0:T(256)S(1)}, s32[256]{0:T(256)}, u32[]{:S(2)}) copy-start(s32[256]{0:T(256)} %copy-done.5) | copy-start | bytes 3076
where the time goes:
time: 81.1 us; the launch traced here: 79.4 us
  waiting for transfers between devices  36.2 us (45%)
  starting transfers between devices  20.2 us (25%)
  matrix products  7.86 us (10%)
  Pallas kernels  5.57 us (7%)
  other arithmetic  4.14 us (5%)
  between operations  3.47 us (4%)
  local copies, waits for them, and re-layouts  1.65 us (2%)
    ppermute x4, waiting for transfers between devices, one(): moved = lax.ppermute(moved, 'rep', route)  26.4 us
    ppermute x13, starting transfers between devices, swap(): return lax.ppermute(block, axis, [(i, i ^ bit) for i in range(count)])  11.4 us
    ppermute x13, waiting for transfers between devices, swap(): return lax.ppermute(block, axis, [(i, i ^ bit) for i in range(count)])  9.79 us
    ppermute x4, starting transfers between devices, one(): moved = lax.ppermute(moved, 'rep', route)  8.85 us
    pallas_call x1, Pallas kernels, head_gradient(): pl.pallas_call(head_kernel, grid=(vocab // step,), out_shape=jax.ShapeDty...  4.13 us
    dot_general x3, matrix products, partial_state(): jnp.einsum('rv,wv->rw', gradient, head_weight, preferred_element_type=jnp...  3.02 us
    convert_element_type x2, other arithmetic, difference(): return (distill_weight * spread).astype(jnp.bfloat16)  2.38 us
  transfers between devices with their start and end apart: 17, of which 12 were waited for; matrix products, arithmetic and copies ran while one was open for 6% of the time, Pallas kernels for 7%

commit v1 on v0

--- a/solution.py
+++ b/solution.py
@@ -255,11 +255,6 @@
         logits.append((home, far))
     sib = swap(logits[0][1], "rep", 2)
     codes = routes(after(pair_order, *logits[-1]), head_weight.shape[1])
-    chip_rows = jnp.einsum(
-        "mei,miw->mew", onehot_chip, after(states, *logits[0]), preferred_element_type=jnp.float32
-    )
-    chip_rows = chip_rows.astype(jnp.bfloat16)
-
     def settle(home, sib, first, second, to_home_first):
         grad_home = difference(home, jnp.where(to_home_first, first, second))
         grad_sib = difference(sib, jnp.where(to_home_first, second, first))
@@ -268,16 +263,10 @@
     def leaving(home, sib, home_first):
         return jnp.where(home_first, home, sib), jnp.where(home_first, sib, home)
 
-    def partial_state(*blocks):
+    def partial_state(heads, *blocks):
         gradient = jnp.concatenate(blocks, axis=0)
-        partial = jnp.einsum(
-            "rv,wv->rw", gradient, head_weight, preferred_element_type=jnp.float32
-        )
+        partial = jnp.einsum("rv,wv->rw", gradient, heads, preferred_element_type=jnp.float32)
         return partial, partial.astype(jnp.bfloat16)
-
-    def whole_state(partial, sent, *before):
-        other = after(swap(sent, "voc", 1), *before).astype(jnp.float32)
-        return (partial + other).astype(jnp.bfloat16)
 
     def beside(nexts, settled):
         arriving = [swap(far, "rep", 2) for far in nexts]
@@ -292,9 +281,7 @@
         branches, (home_first, to_home_first) = codes[m]
         sent = leaving(home, sib, home_first)
         nexts = [] if m + 1 == micro_count else [logits[m + 1][1]]
-        if m == 0:
-            sent = [after(block, chip_rows) for block in sent]
-        else:
+        if m > 0:
             sent = [after(block, *settled[0]) for block in sent]
         first, (arriving, returned) = move_pairs(
             sent[0], branches[0], pairs, beside, nexts, settled
@@ -310,16 +297,28 @@
     [(grad_home, grad_sib)] = settled
     far = swap(grad_sib, "rep", 2)
     near = swap(grad_home, "rep", 1)
+    heads = after(head_weight, grad_sib)
     early = [[after(block, near) for block in group] for group in early]
-    parts = [partial_state(*group) for group in [*early, (grad_home, near)]]
-    far = after(far, *[sent for _, sent in parts])
+    chip_rows = jnp.einsum(
+        "mei,miw->mew", onehot_chip, after(states, near), preferred_element_type=jnp.float32
+    )
+    chip_rows = chip_rows.astype(jnp.bfloat16)
+    parts = [partial_state(heads, *group) for group in early]
+    early_other = [swap(sent, "voc", 1) for _, sent in parts]
+    near_part = partial_state(heads, grad_home, near)
+    far = after(far, near_part[1], *early_other)
     farther = swap(far, "rep", 1)
+    far_part = partial_state(heads, far, farther)
     head_grad = head_gradient(
         chip_rows.reshape(micro_count * row_count, half_width),
         sum(early, []) + [grad_home, near, far, farther],
     )
-    canon = [whole_state(*part, head_grad) for part in parts[:-1]]
-    last = [whole_state(*parts[-1]), whole_state(*partial_state(far, farther))]
+
+    def whole_state(partial, other):
+        return (partial + other.astype(jnp.float32)).astype(jnp.bfloat16)
+
+    canon = [whole_state(part[0], other) for part, other in zip(parts, early_other)]
+    last = [whole_state(part[0], swap(part[1], "voc", 1)) for part in (near_part, far_part)]
     canon.append(jnp.concatenate(last, axis=0))
     state_grad = jnp.einsum(
         "mei,mew->miw", onehot_chip, jnp.stack(canon), preferred_element_type=jnp.float32

time: 81.1 us -> 79 us (0.974); the launches traced: 79.4 us -> 79.8 us
  starting transfers between devices: 20.2 us -> 23.2 us
  waiting for transfers between devices: 36.2 us -> 34.6 us
  other arithmetic: 4.14 us -> 3.09 us
    ppermute x4, waiting for transfers between devices: 26.4 us -> 23.8 us  [one(): moved = lax.ppermute(moved, 'rep', route)]
    ppermute x4, starting transfers between devices: 8.85 us -> 10.5 us  [one(): moved = lax.ppermute(moved, 'rep', route)]
    ppermute x13, starting transfers between devices: 11.4 us -> 12.7 us  [swap(): return lax.ppermute(block, axis, [(i, i ^ bit) for i in range(count)])]
    ppermute x13, waiting for transfers between devices: 9.79 us -> 10.8 us  [swap(): return lax.ppermute(block, axis, [(i, i ^ bit) for i in range(count)])]
    convert_element_type x2, other arithmetic: 2.38 us -> 1.43 us  [difference(): return (distill_weight * spread).astype(jnp.bfloat16)]
where the time goes in v1:
time: 79 us; the launch traced here: 79.8 us
  waiting for transfers between devices  34.6 us (44%)
  starting transfers between devices  23.2 us (29%)
  matrix products  7.75 us (10%)
  Pallas kernels  5.6 us (7%)
  between operations  3.45 us (4%)
  other arithmetic  3.09 us (4%)
  local copies, waits for them, and re-layouts  1.64 us (2%)
    ppermute x4, waiting for transfers between devices, one(): moved = lax.ppermute(moved, 'rep', route)  23.8 us
    ppermute x13, starting transfers between devices, swap(): return lax.ppermute(block, axis, [(i, i ^ bit) for i in range(count)])  12.7 us
    ppermute x13, waiting for transfers between devices, swap(): return lax.ppermute(block, axis, [(i, i ^ bit) for i in range(count)])  10.8 us
    ppermute x4, starting transfers between devices, one(): moved = lax.ppermute(moved, 'rep', route)  10.5 us
    pallas_call x1, Pallas kernels, head_gradient(): pl.pallas_call(head_kernel, grid=(vocab // step,), out_shape=jax.ShapeDty...  4.16 us
    dot_general x3, matrix products, partial_state(): jnp.einsum('rv,wv->rw', gradient, heads, preferred_element_type=jnp.float32)  3.03 us
  transfers between devices with their start and end apart: 17, of which 12 were waited for; matrix products, arithmetic and copies ran while one was open for 6% of the time, Pallas kernels for 7%

profile of v1, /device:TPU:0, one launch (start us, length us, event | category | flops | bytes accessed | tf_op | source)
XLA Modules:
  0.0 79.8 jit_solution(9920126150181110182)
XLA Ops:
  0.7 0.8 %constant_dynamic-slice_fusion = s32[2,1,256]{2,1,0:T(1,128)S(1)} fusion(s32[2,8,256]{2,1,0:T(8,128)} %param.103, s32[]{:T(128)S(6)} %select_n.80), kind=kLoop, calls=%fused_computation.79 | loop fusion | bytes 4100 | tf_op jit(solution)/shard_map/jit(dynamic_index_in_dim)/dynamic_slice | solution.py:235
  1.7 1.2 %convolution_convert_fusion.3 = bf16[256,384]{1,0:T(8,128)(2,1)S(1)} fusion(pred[2,256,256]{2,1,0:T(32,128)(4,1)S(1)} %broadcast_compare_fusion, bf16[2,256,384]{2,1,0:T(8,128)(2,1)} %param.100), kind=kOutput, calls=%fused_computation.3 | convolution fusion | flops 50429952 | bytes 458752 | tf_op jit(solution)/shard_map/dot_general | solution.py:248
  6.2 3.0 %collective-permute-start.190 = (bf16[64,2048]{1,0:T(8,128)(2,1)S(1)}, bf16[64,2048]{1,0:T(8,128)(2,1)S(1)}, u32[]{:S(2)}, u32[]{:S(2)}) collective-permute-start(bf16[64,2048]{1,0:T(8,128)(2,1)S(1)} %fusion.10), channel_id=1, source_target_pairs={{0,4},{2,6},{4,0},{6,2},{8,12},{10,14},{12,8},{14,10},{16,20},{18,... | collective-permute-start | bytes 786440 | tf_op jit(solution)/shard_map/ppermute | solution.py:89
  9.3 1.4 %shard_map.59 = (s32[1]{0:T(128)}, s32[1]{0:T(128)}, s32[1]{0:T(128)}, s32[1]{0:T(128)}, s32[4,2048]{1,0:T(4,128)S(1)}) custom-call(s32[2,8]{1,0:T(2,128)S(1)} %copy-done.1), custom_call_target="tpu_custom_call" | custom-call | tf_op jit(solution)/shard_map/pallas_call | solution.py:62
  13.4 2.4 %collective-permute-done.190 = bf16[64,2048]{1,0:T(8,128)(2,1)S(1)} collective-permute-done((bf16[64,2048]{1,0:T(8,128)(2,1)S(1)}, bf16[64,2048]{1,0:T(8,128)(2,1)S(1)}, u32[]{:S(2)}, u32[]{:S(2)}) %collective-permute-start.190) | collective-permute-done | bytes 262176 | tf_op jit(solution)/shard_map/ppermute | solution.py:89
  16.0 12.2 %conditional.4 = (bf16[64,2048]{1,0:T(8,128)(2,1)S(1)}, bf16[64,2048]{1,0:T(8,128)(2,1)}) conditional(s32[]{:T(128)} %bitcast.4, (bf16[64,2048]{1,0:T(8,128)(2,1)S(1)}, bf16[64,2048]{1,0:T(8,128)(2,1)S(1)}) %tuple.381, (bf16[64,2048]{1,0:T(8,128)(2,1)S(1)}, bf16[64,2048]{1,0:T(8,128)(2,1)S(1)}) %tuple.382, ...), branch_computations={%region_0.1_spmd, %region_1.2_spmd, %region_2.3_spmd, %region_3.4_... | conditional | bytes 2621536 | solution.py:84
  16.0 4.7 %collective-permute-start.27 = (bf16[64,2048]{1,0:T(8,128)(2,1)S(1)}, bf16[64,2048]{1,0:T(8,128)(2,1)S(1)}, u32[]{:S(2)}, u32[]{:S(2)}) collective-permute-start(bf16[64,2048]{1,0:T(8,128)(2,1)S(1)} %get-tuple-element.413), channel_id=1, source_target_pairs={{0,16},{2,18},{4,20},{6,22},{8,8},{10,10},{12,12},{14,14},{16,0},{... | collective-permute-start | bytes 786440 | tf_op jit(solution)/shard_map/cond/branch_14_fun/ppermute | solution.py:80
  20.7 1.6 %collective-permute-start.28 = (bf16[64,2048]{1,0:T(8,128)(2,1)S(1)}, bf16[64,2048]{1,0:T(8,128)(2,1)}, u32[]{:S(2)}, u32[]{:S(2)}) collective-permute-start(bf16[64,2048]{1,0:T(8,128)(2,1)S(1)} %get-tuple-element.414), channel_id=1, source_target_pairs={{0,4},{2,6},{4,0},{6,2},{8,12},{10,14},{12,8},{14,10},{16,20},{18,... | collective-permute-start | bytes 786440 | tf_op jit(solution)/shard_map/cond/branch_14_fun/ppermute | solution.py:89
  22.3 4.3 %collective-permute-done.27 = bf16[64,2048]{1,0:T(8,128)(2,1)S(1)} collective-permute-done((bf16[64,2048]{1,0:T(8,128)(2,1)S(1)}, bf16[64,2048]{1,0:T(8,128)(2,1)S(1)}, u32[]{:S(2)}, u32[]{:S(2)}) %collective-permute-start.27) | collective-permute-done | bytes 262176 | tf_op jit(solution)/shard_map/cond/branch_14_fun/ppermute | solution.py:80
  26.7 1.5 %collective-permute-done.28 = bf16[64,2048]{1,0:T(8,128)(2,1)} collective-permute-done((bf16[64,2048]{1,0:T(8,128)(2,1)S(1)}, bf16[64,2048]{1,0:T(8,128)(2,1)}, u32[]{:S(2)}, u32[]{:S(2)}) %collective-permute-start.28) | collective-permute-done | bytes 262176 | tf_op jit(solution)/shard_map/cond/branch_14_fun/ppermute | solution.py:89
  28.1 11.0 %conditional.5 = (bf16[64,2048]{1,0:T(8,128)(2,1)S(1)}) conditional(s32[]{:T(128)} %bitcast.5, bf16[64,2048]{1,0:T(8,128)(2,1)S(1)} %get-tuple-element.584, bf16[64,2048]{1,0:T(8,128)(2,1)S(1)} %get-tuple-element.584, bf16[64,2048]{1,0:T(8,128)(2,1)S(1)} %get-tuple-element.584, ...), branch_computations={%region_24.25_spmd, %region_25.26_spmd, %region_26.27_spmd, %regio... | conditional | bytes 1572912 | solution.py:84
  28.1 1.9 %collective-permute-start.57 = (bf16[64,2048]{1,0:T(8,128)(2,1)S(1)}, bf16[64,2048]{1,0:T(8,128)(2,1)S(1)}, u32[]{:S(2)}, u32[]{:S(2)}) collective-permute-start(bf16[64,2048]{1,0:T(8,128)(2,1)S(1)} %param.35), channel_id=1, source_target_pairs={{0,8},{2,10},{4,12},{6,14},{8,24},{10,26},{12,28},{14,30},{16,16},... | collective-permute-start | bytes 786440 | tf_op jit(solution)/shard_map/cond/branch_11_fun/ppermute | solution.py:80
  30.1 9.0 %collective-permute-done.57 = bf16[64,2048]{1,0:T(8,128)(2,1)S(1)} collective-permute-done((bf16[64,2048]{1,0:T(8,128)(2,1)S(1)}, bf16[64,2048]{1,0:T(8,128)(2,1)S(1)}, u32[]{:S(2)}, u32[]{:S(2)}) %collective-permute-start.57) | collective-permute-done | bytes 262176 | tf_op jit(solution)/shard_map/cond/branch_11_fun/ppermute | solution.py:80
  39.1 1.0 %broadcast_select_fusion = (bf16[64,2048]{1,0:T(8,128)(2,1)S(1)}, bf16[64,2048]{1,0:T(8,128)(2,1)S(1)}) fusion(bf16[64,2048]{1,0:T(8,128)(2,1)} %get-tuple-element.586, bf16[64,2048]{1,0:T(8,128)(2,1)S(1)} %get-tuple-element.610, pred[2048]{0:T(1024)(128)(4,1)S(1)} %get-tuple-element.604), kind=kLoop, calls=%fused_computation.45 | loop fusion | flops 262144 | bytes 1050624 | tf_op jit(solution)/shard_map/jit(_where)/select_n | solution.py:264
  40.3 6.7 %conditional.6 = (bf16[64,2048]{1,0:T(8,128)(2,1)S(1)}, bf16[64,2048]{1,0:T(8,128)(2,1)}) conditional(s32[]{:T(128)} %bitcast.6, (bf16[64,2048]{1,0:T(8,128)(2,1)S(1)}, bf16[64,2048]{1,0:T(8,128)(2,1)S(1)}) %tuple.385, (bf16[64,2048]{1,0:T(8,128)(2,1)S(1)}, bf16[64,2048]{1,0:T(8,128)(2,1)S(1)}) %tuple.386, ...), branch_computations={%region_48.49_spmd, %region_49.50_spmd, %region_50.51_spmd, %regio... | conditional | bytes 2621536 | solution.py:84
  40.4 1.6 %collective-permute-start.84 = (bf16[64,2048]{1,0:T(8,128)(2,1)S(1)}, bf16[64,2048]{1,0:T(8,128)(2,1)}, u32[]{:S(2)}, u32[]{:S(2)}) collective-permute-start(bf16[64,2048]{1,0:T(8,128)(2,1)S(1)} %get-tuple-element.448), channel_id=1, source_target_pairs={{0,4},{2,6},{4,0},{6,2},{8,12},{10,14},{12,8},{14,10},{16,20},{18,... | collective-permute-start | bytes 786440 | tf_op jit(solution)/shard_map/cond/branch_7_fun/ppermute | solution.py:89
  42.0 4.8 %collective-permute-done.83 = bf16[64,2048]{1,0:T(8,128)(2,1)S(1)} collective-permute-done((bf16[64,2048]{1,0:T(8,128)(2,1)S(1)}, bf16[64,2048]{1,0:T(8,128)(2,1)S(1)}, u32[]{:S(2)}, u32[]{:S(2)}) %collective-permute-start.83) | collective-permute-done | bytes 262176 | tf_op jit(solution)/shard_map/cond/branch_7_fun/ppermute | solution.py:80
  47.0 0.7 copy-done.2
  47.7 10.3 %conditional.7 = (bf16[64,2048]{1,0:T(8,128)(2,1)S(1)}, bf16[64,2048]{1,0:T(8,128)(2,1)}, bf16[64,2048]{1,0:T(8,128)(2,1)}) conditional(s32[]{:T(128)} %bitcast.7, (bf16[64,2048]{1,0:T(8,128)(2,1)S(1)}, bf16[64,2048]{1,0:T(8,128)(2,1)}, bf16[64,2048]{1,0:T(8,128)(2,1)S(1)}) %tuple.389, ...), branch_computations={%region_72.73_spmd, %region_73.74_spmd, %region_74.75_spmd, %regio... | conditional | bytes 3670160 | solution.py:84
  47.7 3.8 %collective-permute-start.149 = (bf16[64,2048]{1,0:T(8,128)(2,1)S(1)}, bf16[64,2048]{1,0:T(8,128)(2,1)S(1)}, u32[]{:S(2)}, u32[]{:S(2)}) collective-permute-start(bf16[64,2048]{1,0:T(8,128)(2,1)S(1)} %get-tuple-element.514), channel_id=1, source_target_pairs={{0,8},{2,10},{4,12},{6,14},{8,24},{10,26},{12,28},{14,30},{16,16},... | collective-permute-start | bytes 786440 | tf_op jit(solution)/shard_map/cond/branch_11_fun/ppermute | solution.py:80
  52.1 5.7 %collective-permute-done.149 = bf16[64,2048]{1,0:T(8,128)(2,1)S(1)} collective-permute-done((bf16[64,2048]{1,0:T(8,128)(2,1)S(1)}, bf16[64,2048]{1,0:T(8,128)(2,1)S(1)}, u32[]{:S(2)}, u32[]{:S(2)}) %collective-permute-start.149) | collective-permute-done | bytes 262176 | tf_op jit(solution)/shard_map/cond/branch_11_fun/ppermute | solution.py:80
  58.1 1.2 %multiply_convert_fusion.1 = (bf16[64,2048]{1,0:T(8,128)(2,1)S(1)}, bf16[64,2048]{1,0:T(8,128)(2,1)S(1)}) fusion(bf16[64,2048]{1,0:T(8,128)(2,1)S(1)} %get-tuple-element.610, bf16[64,2048]{1,0:T(8,128)(2,1)} %copy-done.2, bf16[64,2048]{1,0:T(8,128)(2,1)S(1)} %get-tuple-element.593, pred[2048]{0:T(1024)(128)(4,1)S(1)} %get-tuple-element.603, ...), kind=kLoop, calls=%fused_computation.31 | loop fusion | flops 1572864 | bytes 1574912 | tf_op jit(solution)/shard_map/convert_element_type | solution.py:94
  59.4 1.6 %collective-permute-start.194 = (bf16[64,2048]{1,0:T(8,128)(2,1)S(1)}, bf16[64,2048]{1,0:T(8,128)(2,1)S(1)}, u32[]{:S(2)}, u32[]{:S(2)}) collective-permute-start(bf16[64,2048]{1,0:T(8,128)(2,1)S(1)} %get-tuple-element.612), channel_id=1, source_target_pairs={{0,4},{2,6},{4,0},{6,2},{8,12},{10,14},{12,8},{14,10},{16,20},{18,... | collective-permute-start | bytes 786440 | tf_op jit(solution)/shard_map/ppermute | solution.py:89
  61.0 1.8 %fusion.50 = (bf16[256,384]{1,0:T(8,128)(2,1)S(1)}, f32[256,384]{1,0:T(8,128)S(1)}) fusion(bf16[384,2048]{1,0:T(8,128)(2,1)S(1)} %copy-done, bf16[64,2048]{1,0:T(8,128)(2,1)} %get-tuple-element.599.refs_4_, bf16[64,2048]{1,0:T(8,128)(2,1)} %get-tuple-element.597.refs_3_, bf16[64,2048]{1,0:T(8,128)(2,1)} %get-tuple-element.596.refs_2_, ...), kind=kOutput, calls=%fused_computation.85 | convolution fusion | flops 406945792 | bytes 3211264 | tf_op jit(solution)/shard_map/rv,wv->rw/dot_general | solution.py:268
  62.8 1.5 %collective-permute-start.192 = (bf16[256,384]{1,0:T(8,128)(2,1)S(1)}, bf16[256,384]{1,0:T(8,128)(2,1)S(1)}, u32[]{:S(2)}, u32[]{:S(2)}) collective-permute-start(bf16[256,384]{1,0:T(8,128)(2,1)S(1)} %get-tuple-element.619), channel_id=1, source_target_pairs={{0,1},{1,0},{2,3},{3,2},{4,5},{5,4},{6,7},{7,6},{8,9},{9,8},{10,11... | collective-permute-start | bytes 589832 | tf_op jit(solution)/shard_map/ppermute | solution.py:89
  65.0 0.6 collective-permute-start.193
  65.6 2.5 %collective-permute-done.194.refs_7_ = bf16[64,2048]{1,0:T(8,128)(2,1)S(1)} collective-permute-done((bf16[64,2048]{1,0:T(8,128)(2,1)S(1)}, bf16[64,2048]{1,0:T(8,128)(2,1)S(1)}, u32[]{:S(2)}, u32[]{:S(2)}) %collective-permute-start.194) | collective-permute-done | bytes 262176 | tf_op jit(solution)/shard_map/ppermute | solution.py:89
  68.1 2.5 %collective-permute-done.192 = bf16[256,384]{1,0:T(8,128)(2,1)S(1)} collective-permute-done((bf16[256,384]{1,0:T(8,128)(2,1)S(1)}, bf16[256,384]{1,0:T(8,128)(2,1)S(1)}, u32[]{:S(2)}, u32[]{:S(2)}) %collective-permute-start.192) | collective-permute-done | bytes 196640 | tf_op jit(solution)/shard_map/ppermute | solution.py:89
  71.0 1.0 %collective-permute-done.193 = bf16[128,384]{1,0:T(8,128)(2,1)S(1)} collective-permute-done((bf16[128,384]{1,0:T(8,128)(2,1)S(1)}, bf16[128,384]{1,0:T(8,128)(2,1)S(1)}, u32[]{:S(2)}, u32[]{:S(2)}) %collective-permute-start.193) | collective-permute-done | bytes 98336 | tf_op jit(solution)/shard_map/ppermute | solution.py:89
  72.8 1.5 %collective-permute-start.196 = (bf16[128,384]{1,0:T(8,128)(2,1)S(1)}, bf16[128,384]{1,0:T(8,128)(2,1)S(1)}, u32[]{:S(2)}, u32[]{:S(2)}) collective-permute-start(bf16[128,384]{1,0:T(8,128)(2,1)S(1)} %get-tuple-element.621), channel_id=1, source_target_pairs={{0,1},{1,0},{2,3},{3,2},{4,5},{5,4},{6,7},{7,6},{8,9},{9,8},{10,11... | collective-permute-start | bytes 294920 | tf_op jit(solution)/shard_map/ppermute | solution.py:89
  74.4 4.2 %shard_map.60 = bf16[384,2048]{1,0:T(8,128)(2,1)} custom-call(bf16[512,384]{1,0:T(8,128)(2,1)S(1)} %bitcast.32, bf16[64,2048]{1,0:T(8,128)(2,1)S(1)} %get-tuple-element.594.refs_1_, bf16[64,2048]{1,0:T(8,128)(2,1)} %get-tuple-element.596.refs_2_, bf16[64,2048]{1,0:T(8,128)(2,1)} %get-tuple-element.597.refs_3_, bf16[64,2048]{1,0:T(8,128)(2,1)} %get-tuple-element.599.refs_4_, ...), custom_call_target="tpu_custom_call" | custom-call | flops 805306368 | bytes 4063232 | tf_op jit(solution)/shard_map/pallas_call | solution.py:207
  78.6 1.2 %convolution_convert_fusion.1 = bf16[2,256,384]{2,1,0:T(8,128)(2,1)} fusion(bf16[1,256,384]{2,1,0:T(8,128)(2,1)S(1)} %maximum_bitcast_fusion, bf16[1,256,384]{2,1,0:T(8,128)(2,1)S(1)} %fusion.29, s32[2,256]{1,0:T(2,128)S(1)} %bitcast.35, s32[256]{0:T(256)S(1)} %add_add_fusion.1), kind=kOutput, calls=%fused_computation.1 | convolution fusion | flops 101187584 | bytes 789504 | tf_op jit(solution)/shard_map/mei,mew->miw/dot_general | solution.py:323
  (50 shorter events, 6.8 us)
Async XLA Ops:
  0.6 2.3 %copy-start = (bf16[384,2048]{1,0:T(8,128)(2,1)S(1)}, bf16[384,2048]{1,0:T(8,128)(2,1)}, u32[]{:S(2)}) copy-start(bf16[384,2048]{1,0:T(8,128)(2,1)} %param.101) | copy-start | bytes 4718596
  1.7 2.2 %copy-start.3 = (bf16[2,256,384]{2,1,0:T(8,128)(2,1)S(1)}, bf16[2,256,384]{2,1,0:T(8,128)(2,1)}, u32[]{:S(2)}) copy-start(bf16[2,256,384]{2,1,0:T(8,128)(2,1)} %param.100) | copy-start | bytes 1179652
  3.4 2.8 %collective-permute-start.188 = (f32[128,2048]{1,0:T(8,128)S(1)}, f32[128,2048]{1,0:T(8,128)S(1)}, u32[]{:S(2)}, u32[]{:S(2)}) collective-permute-start(f32[128,2048]{1,0:T(8,128)S(1)} %fusion.38), channel_id=1, source_target_pairs={{0,2},{2,0},{4,6},{6,4},{8,10},{10,8},{12,14},{14,12},{16,18},{18,... | collective-permute-start | bytes 3145736 | tf_op jit(solution)/shard_map/ppermute | solution.py:89
  4.6 4.6 %collective-permute-start.189 = (f32[128,2048]{1,0:T(8,128)S(1)}, f32[128,2048]{1,0:T(8,128)S(1)}, u32[]{:S(2)}, u32[]{:S(2)}) collective-permute-start(f32[128,2048]{1,0:T(8,128)S(1)} %fusion.34), channel_id=1, source_target_pairs={{0,2},{2,0},{4,6},{6,4},{8,10},{10,8},{12,14},{14,12},{16,18},{18,... | collective-permute-start | bytes 3145736 | tf_op jit(solution)/shard_map/ppermute | solution.py:89
  6.2 3.1 %copy-start.1 = (s32[2,8]{1,0:T(2,128)S(1)}, s32[2,8]{1,0:T(2,128)}, u32[]{:S(2)}) copy-start(s32[2,8]{1,0:T(2,128)} %order_ref) | copy-start | bytes 196
  6.2 9.6 %collective-permute-start.190 = (bf16[64,2048]{1,0:T(8,128)(2,1)S(1)}, bf16[64,2048]{1,0:T(8,128)(2,1)S(1)}, u32[]{:S(2)}, u32[]{:S(2)}) collective-permute-start(bf16[64,2048]{1,0:T(8,128)(2,1)S(1)} %fusion.10), channel_id=1, source_target_pairs={{0,4},{2,6},{4,0},{6,2},{8,12},{10,14},{12,8},{14,10},{16,20},{18,... | collective-permute-start | bytes 786440 | tf_op jit(solution)/shard_map/ppermute | solution.py:89
  16.0 10.6 %collective-permute-start.27 = (bf16[64,2048]{1,0:T(8,128)(2,1)S(1)}, bf16[64,2048]{1,0:T(8,128)(2,1)S(1)}, u32[]{:S(2)}, u32[]{:S(2)}) collective-permute-start(bf16[64,2048]{1,0:T(8,128)(2,1)S(1)} %get-tuple-element.413), channel_id=1, source_target_pairs={{0,16},{2,18},{4,20},{6,22},{8,8},{10,10},{12,12},{14,14},{16,0},{... | collective-permute-start | bytes 786440 | tf_op jit(solution)/shard_map/cond/branch_14_fun/ppermute | solution.py:80
  20.7 7.4 %collective-permute-start.28 = (bf16[64,2048]{1,0:T(8,128)(2,1)S(1)}, bf16[64,2048]{1,0:T(8,128)(2,1)}, u32[]{:S(2)}, u32[]{:S(2)}) collective-permute-start(bf16[64,2048]{1,0:T(8,128)(2,1)S(1)} %get-tuple-element.414), channel_id=1, source_target_pairs={{0,4},{2,6},{4,0},{6,2},{8,12},{10,14},{12,8},{14,10},{16,20},{18,... | collective-permute-start | bytes 786440 | tf_op jit(solution)/shard_map/cond/branch_14_fun/ppermute | solution.py:89
  28.1 10.9 %collective-permute-start.57 = (bf16[64,2048]{1,0:T(8,128)(2,1)S(1)}, bf16[64,2048]{1,0:T(8,128)(2,1)S(1)}, u32[]{:S(2)}, u32[]{:S(2)}) collective-permute-start(bf16[64,2048]{1,0:T(8,128)(2,1)S(1)} %param.35), channel_id=1, source_target_pairs={{0,8},{2,10},{4,12},{6,14},{8,24},{10,26},{12,28},{14,30},{16,16},... | collective-permute-start | bytes 786440 | tf_op jit(solution)/shard_map/cond/branch_11_fun/ppermute | solution.py:80
  40.4 6.4 %collective-permute-start.83 = (bf16[64,2048]{1,0:T(8,128)(2,1)S(1)}, bf16[64,2048]{1,0:T(8,128)(2,1)S(1)}, u32[]{:S(2)}, u32[]{:S(2)}) collective-permute-start(bf16[64,2048]{1,0:T(8,128)(2,1)S(1)} %get-tuple-element.447), channel_id=1, source_target_pairs={{0,8},{2,10},{4,12},{6,14},{8,0},{10,2},{12,4},{14,6},{16,24},{18,... | collective-permute-start | bytes 786440 | tf_op jit(solution)/shard_map/cond/branch_7_fun/ppermute | solution.py:80
  40.4 6.5 %collective-permute-start.84 = (bf16[64,2048]{1,0:T(8,128)(2,1)S(1)}, bf16[64,2048]{1,0:T(8,128)(2,1)}, u32[]{:S(2)}, u32[]{:S(2)}) collective-permute-start(bf16[64,2048]{1,0:T(8,128)(2,1)S(1)} %get-tuple-element.448), channel_id=1, source_target_pairs={{0,4},{2,6},{4,0},{6,2},{8,12},{10,14},{12,8},{14,10},{16,20},{18,... | collective-permute-start | bytes 786440 | tf_op jit(solution)/shard_map/cond/branch_7_fun/ppermute | solution.py:89
  47.0 0.7 copy-start.2
  47.7 10.1 %collective-permute-start.149 = (bf16[64,2048]{1,0:T(8,128)(2,1)S(1)}, bf16[64,2048]{1,0:T(8,128)(2,1)S(1)}, u32[]{:S(2)}, u32[]{:S(2)}) collective-permute-start(bf16[64,2048]{1,0:T(8,128)(2,1)S(1)} %get-tuple-element.514), channel_id=1, source_target_pairs={{0,8},{2,10},{4,12},{6,14},{8,24},{10,26},{12,28},{14,30},{16,16},... | collective-permute-start | bytes 786440 | tf_op jit(solution)/shard_map/cond/branch_11_fun/ppermute | solution.py:80
  51.5 6.3 %collective-permute-start.150 = (bf16[64,2048]{1,0:T(8,128)(2,1)S(1)}, bf16[64,2048]{1,0:T(8,128)(2,1)}, u32[]{:S(2)}, u32[]{:S(2)}) collective-permute-start(bf16[64,2048]{1,0:T(8,128)(2,1)S(1)} %get-tuple-element.515), channel_id=1, source_target_pairs={{0,2},{2,0},{4,6},{6,4},{8,10},{10,8},{12,14},{14,12},{16,18},{18,... | collective-permute-start | bytes 786440 | tf_op jit(solution)/shard_map/cond/branch_11_fun/ppermute | solution.py:89
  51.6 6.2 %collective-permute-start.151 = (bf16[64,2048]{1,0:T(8,128)(2,1)}, bf16[64,2048]{1,0:T(8,128)(2,1)}, u32[]{:S(2)}, u32[]{:S(2)}) collective-permute-start(bf16[64,2048]{1,0:T(8,128)(2,1)} %get-tuple-element.516), channel_id=1, source_target_pairs={{0,2},{2,0},{4,6},{6,4},{8,10},{10,8},{12,14},{14,12},{16,18},{18,... | collective-permute-start | bytes 786440 | tf_op jit(solution)/shard_map/cond/branch_11_fun/ppermute | solution.py:89
  59.3 1.7 %collective-permute-start.191 = (bf16[64,2048]{1,0:T(8,128)(2,1)S(1)}, bf16[64,2048]{1,0:T(8,128)(2,1)S(1)}, u32[]{:S(2)}, u32[]{:S(2)}) collective-permute-start(bf16[64,2048]{1,0:T(8,128)(2,1)S(1)} %get-tuple-element.611.refs_5_), channel_id=1, source_target_pairs={{0,2},{2,0},{4,6},{6,4},{8,10},{10,8},{12,14},{14,12},{16,18},{18,... | collective-permute-start | bytes 786440 | tf_op jit(solution)/shard_map/ppermute | solution.py:89
  59.4 8.7 %collective-permute-start.194 = (bf16[64,2048]{1,0:T(8,128)(2,1)S(1)}, bf16[64,2048]{1,0:T(8,128)(2,1)S(1)}, u32[]{:S(2)}, u32[]{:S(2)}) collective-permute-start(bf16[64,2048]{1,0:T(8,128)(2,1)S(1)} %get-tuple-element.612), channel_id=1, source_target_pairs={{0,4},{2,6},{4,0},{6,2},{8,12},{10,14},{12,8},{14,10},{16,20},{18,... | collective-permute-start | bytes 786440 | tf_op jit(solution)/shard_map/ppermute | solution.py:89
  62.8 7.8 %copy-start.4 = (bf16[2,256,384]{2,1,0:T(8,128)(2,1)S(1)}, bf16[2,256,384]{2,1,0:T(8,128)(2,1)}, u32[]{:S(2)}) copy-start(bf16[2,256,384]{2,1,0:T(8,128)(2,1)} %param.100) | copy-start | bytes 1179652
  62.8 7.8 %collective-permute-start.192 = (bf16[256,384]{1,0:T(8,128)(2,1)S(1)}, bf16[256,384]{1,0:T(8,128)(2,1)S(1)}, u32[]{:S(2)}, u32[]{:S(2)}) collective-permute-start(bf16[256,384]{1,0:T(8,128)(2,1)S(1)} %get-tuple-element.619), channel_id=1, source_target_pairs={{0,1},{1,0},{2,3},{3,2},{4,5},{5,4},{6,7},{7,6},{8,9},{9,8},{10,11... | collective-permute-start | bytes 589832 | tf_op jit(solution)/shard_map/ppermute | solution.py:89
  65.0 7.0 %collective-permute-start.193 = (bf16[128,384]{1,0:T(8,128)(2,1)S(1)}, bf16[128,384]{1,0:T(8,128)(2,1)S(1)}, u32[]{:S(2)}, u32[]{:S(2)}) collective-permute-start(bf16[128,384]{1,0:T(8,128)(2,1)S(1)} %get-tuple-element.617), channel_id=1, source_target_pairs={{0,1},{1,0},{2,3},{3,2},{4,5},{5,4},{6,7},{7,6},{8,9},{9,8},{10,11... | collective-permute-start | bytes 294920 | tf_op jit(solution)/shard_map/ppermute | solution.py:89
  70.7 1.5 %collective-permute-start.195 = (bf16[64,2048]{1,0:T(8,128)(2,1)S(1)}, bf16[64,2048]{1,0:T(8,128)(2,1)S(1)}, u32[]{:S(2)}, u32[]{:S(2)}) collective-permute-start(bf16[64,2048]{1,0:T(8,128)(2,1)S(1)} %collective-permute-done.194.refs_7_), channel_id=1, source_target_pairs={{0,2},{2,0},{4,6},{6,4},{8,10},{10,8},{12,14},{14,12},{16,18},{18,... | collective-permute-start | bytes 786440 | tf_op jit(solution)/shard_map/ppermute | solution.py:89
  72.8 5.8 %collective-permute-start.196 = (bf16[128,384]{1,0:T(8,128)(2,1)S(1)}, bf16[128,384]{1,0:T(8,128)(2,1)S(1)}, u32[]{:S(2)}, u32[]{:S(2)}) collective-permute-start(bf16[128,384]{1,0:T(8,128)(2,1)S(1)} %get-tuple-element.621), channel_id=1, source_target_pairs={{0,1},{1,0},{2,3},{3,2},{4,5},{5,4},{6,7},{7,6},{8,9},{9,8},{10,11... | collective-permute-start | bytes 294920 | tf_op jit(solution)/shard_map/ppermute | solution.py:89
